TPU v7x, 256 devices: a whole 4x4x8 slice. The times are simulated.
256 devices in a mesh: ctx: 256 (over z, y, x, core).
Axes of the slice: x: 4, y: 4, z: 8, core: 2. Of those that a mesh axis runs over, the one named last changes fastest.
Arguments:
- query_rows: bfloat16 [32768, 128], P('ctx'), may hold values from -6 to 6
- key_rows: bfloat16 [32768, 128], P('ctx'), may hold values from -6 to 6
- value_rows: bfloat16 [32768, 128], P('ctx'), may hold values from -6 to 6
- saved_out: bfloat16 [32768, 128], P('ctx'), may hold values from -6 to 6
- grad_out: bfloat16 [32768, 128], P('ctx')
- saved_lse: bfloat16 [32768], P('ctx'), as said below
Outputs:
- grad_query: bfloat16 [32768, 128], P('ctx')
- grad_key: bfloat16 [32768, 128], P('ctx')
- grad_value: bfloat16 [32768, 128], P('ctx')
Inputs may be any that keep to these rules, and one draw needn't show every extreme that they name: `saved_lse`: each entry lies within 0.8 of ln(32768) + 0.5.
All inputs are finite; a program needn't handle non-finite values.
Results may differ from a plain program's by a relative error of at most 0.0084.
Values may be sent and summed in bfloat16 or wider, within the bound.
A program may use at most 192 MiB of HBM per device.

v0:
```python
import jax
import jax.numpy as jnp
from jax import lax
from jax.sharding import PartitionSpec as P

HEAD = 128


def score_grads(query_part, lse_part, delta_part, grad_part, keys, values, factor):
    logits = jnp.dot(query_part, keys.T, preferred_element_type=jnp.float32) * factor
    weights = jnp.exp(logits - lse_part.astype(jnp.float32)[:, None])
    grad_prob = jnp.dot(grad_part, values.T, preferred_element_type=jnp.float32)
    grad_score = (weights * (grad_prob - delta_part.astype(jnp.float32)[:, None])).astype(
        jnp.bfloat16
    )
    return (grad_score, weights)


def on_device(query_rows, key_rows, value_rows, saved_out, grad_out, saved_lse):
    factor = HEAD ** (-0.5)
    row_delta = jnp.sum(
        grad_out.astype(jnp.float32) * saved_out.astype(jnp.float32), axis=1
    ).astype(jnp.bfloat16)
    key_piece = lax.all_gather(key_rows, "ctx", axis=0, tiled=True)
    value_piece = lax.all_gather(value_rows, "ctx", axis=0, tiled=True)
    grad_score, weights = score_grads(
        query_rows, saved_lse, row_delta, grad_out, key_piece, value_piece, factor
    )
    query_sum = jnp.dot(grad_score, key_piece, preferred_element_type=jnp.float32)
    query_piece = lax.all_gather(query_rows, "ctx", axis=0, tiled=True)
    grad_piece = lax.all_gather(grad_out, "ctx", axis=0, tiled=True)
    lse_piece = lax.all_gather(saved_lse, "ctx", axis=0, tiled=True)
    delta_piece = lax.all_gather(row_delta, "ctx", axis=0, tiled=True)
    grad_score, weights = score_grads(
        query_piece, lse_piece, delta_piece, grad_piece, key_rows, value_rows, factor
    )
    key_next = jnp.dot(grad_score.T, query_piece, preferred_element_type=jnp.float32)
    value_next = jnp.dot(
        weights.astype(jnp.bfloat16).T, grad_piece, preferred_element_type=jnp.float32
    )
    grad_query = (factor * query_sum).astype(jnp.bfloat16)
    grad_key = (factor * key_next).astype(jnp.bfloat16)
    grad_value = value_next.astype(jnp.bfloat16)
    return (grad_query, grad_key, grad_value)


def solution(mesh):
    in_specs = (
        P("ctx", None),
        P("ctx", None),
        P("ctx", None),
        P("ctx", None),
        P("ctx", None),
        P("ctx"),
    )
    out_specs = (P("ctx", None), P("ctx", None), P("ctx", None))
    return jax.shard_map(
        on_device, mesh=mesh, in_specs=in_specs, out_specs=out_specs, check_vma=False
    )
```

profile of v0, /device:TPU:1, one launch (start us, length us, event | category | flops | bytes accessed | tf_op | source)
XLA Modules:
  0.0 509.4 jit_solution(15135271028125855797)
XLA Ops:
  7.2 0.0 all-gather.7.cloned.1.call-start
  7.2 0.7 all-gather.7.cloned.1.call-update
  7.9 0.0 all-gather.11.cloned.1.call-start
  7.9 0.7 all-gather.11.cloned.1.call-update
  8.6 0.0 all-gather.13.cloned.1.call-start
  8.7 0.7 all-gather.13.cloned.1.call-update
  9.4 0.0 all-gather.9.cloned.1.call-start
  9.4 0.5 all-gather.9.cloned.1.call-update
  10.0 0.7 convert_element_type.47
  10.6 61.1 %all-gather = bf16[256,1,128]{2,1,0:T(2,128)(2,1)S(1)} all-gather(bf16[1,1,128]{2,1,0:T(2,128)(2,1)} %bitcast.20), channel_id=1, replica_groups=mesh['ctx'=256] {'ctx'}, dimensions={0}, use_global_device_ids=true | all-gather | bytes 65792 | tf_op jit(solution)/shard_map/all_gather | solution.py:32
  71.7 0.1 convert_element_type.60
  71.9 0.9 multiply_reduce_fusion
  72.8 53.8 %all-gather.1 = bf16[256,1,128]{2,1,0:T(2,128)(2,1)S(1)} all-gather(bf16[1,1,128]{2,1,0:T(2,128)(2,1)S(1)} %bitcast.19), channel_id=1, replica_groups=mesh['ctx'=256] {'ctx'}, dimensions={0}, use_global_device_ids=true | all-gather | bytes 65792 | tf_op jit(solution)/shard_map/all_gather | solution.py:33
  126.6 0.1 convert_element_type.61
  126.7 0.0 copy-start.1
  126.7 7.4 %all-gather.7.cloned.1.call-done = bf16[32768,128]{1,0:T(8,128)(2,1)} async-done(((bf16[128,128]{1,0:T(8,128)(2,1)}), bf16[32768,128]{1,0:T(8,128)(2,1)}) %all-gather.7.cloned.1.call-update) | async-done | bytes 8388624 | tf_op jit(solution)/shard_map/all_gather | solution.py:24
  134.1 11.7 %fusion.2 = f32[128,32768]{1,0:T(8,128)} fusion(bf16[128,128]{1,0:T(8,128)(2,1)} %param.6, bf16[32768,128]{1,0:T(8,128)(2,1)} %all-gather.7.cloned.1.call-done, f32[128]{0:T(128)S(1)} %convert_element_type.47), kind=kOutput, calls=%fused_computation.4 | convolution fusion | flops 1082130432 | bytes 25199104 | tf_op jit(solution)/shard_map/dot_general | solution.py:10
  145.8 106.6 %all-gather.11.cloned.1.call-done = bf16[32768,128]{1,0:T(8,128)(2,1)} async-done(((bf16[128,128]{1,0:T(8,128)(2,1)}), bf16[32768,128]{1,0:T(8,128)(2,1)}) %all-gather.11.cloned.1.call-update) | async-done | bytes 8388624 | tf_op jit(solution)/shard_map/all_gather | solution.py:30
  252.4 0.0 copy-done.1
  252.4 16.5 %fusion.7 = f32[32768,128]{1,0:T(8,128)} fusion(bf16[32768,128]{1,0:T(8,128)(2,1)} %all-gather.11.cloned.1.call-done, bf16[128,128]{1,0:T(8,128)(2,1)S(1)} %copy-done.1, f32[32768]{0:T(1024)S(1)} %bitcast.17), kind=kOutput, calls=%fused_computation.11 | convolution fusion | flops 1082130432 | bytes 25329664 | tf_op jit(solution)/shard_map/dot_general | solution.py:10
  268.9 0.0 copy-start.2
  268.9 102.0 %all-gather.13.cloned.1.call-done = bf16[32768,128]{1,0:T(8,128)(2,1)} async-done(((bf16[128,128]{1,0:T(8,128)(2,1)}), bf16[32768,128]{1,0:T(8,128)(2,1)}) %all-gather.13.cloned.1.call-update) | async-done | bytes 8388624 | tf_op jit(solution)/shard_map/all_gather | solution.py:31
  370.9 11.2 %fusion.16 = bf16[128,128]{1,0:T(8,128)(2,1)} fusion(bf16[32768,128]{1,0:T(8,128)(2,1)} %all-gather.13.cloned.1.call-done, f32[32768,128]{1,0:T(8,128)} %fusion.7), kind=kOutput, calls=%fused_computation.20 | convolution fusion | flops 1077952512 | bytes 25198592 | tf_op jit(solution)/shard_map/dot_general | solution.py:38
  382.1 0.0 copy-done.2
  382.1 0.0 copy-start
  382.1 20.5 %fusion.14 = bf16[128,128]{1,0:T(8,128)(2,1)} fusion(bf16[32768,128]{1,0:T(8,128)(2,1)} %all-gather.11.cloned.1.call-done, f32[32768,128]{1,0:T(8,128)} %fusion.7, bf16[32768,128]{1,0:T(8,128)(2,1)} %all-gather.13.cloned.1.call-done, bf16[128,128]{1,0:T(8,128)(2,1)S(1)} %copy-done.2, f32[32768]{0:T(1024)S(1)} %bitcast.18), kind=kOutput, calls=%fused_computation.18 | convolution fusion | flops 2160099328 | bytes 33751040 | tf_op jit(solution)/shard_map/dot_general | solution.py:37
  402.7 86.7 %all-gather.9.cloned.1.call-done = bf16[32768,128]{1,0:T(8,128)(2,1)} async-done(((bf16[128,128]{1,0:T(8,128)(2,1)}), bf16[32768,128]{1,0:T(8,128)(2,1)}) %all-gather.9.cloned.1.call-update) | async-done | bytes 8388624 | tf_op jit(solution)/shard_map/all_gather | solution.py:25
  489.3 0.0 copy-done
  489.3 13.5 %fusion.15 = bf16[128,128]{1,0:T(8,128)(2,1)} fusion(bf16[32768,128]{1,0:T(8,128)(2,1)} %all-gather.7.cloned.1.call-done, f32[128,32768]{1,0:T(8,128)} %fusion.2, bf16[128,128]{1,0:T(8,128)(2,1)S(1)} %copy-done, bf16[32768,128]{1,0:T(8,128)(2,1)} %all-gather.9.cloned.1.call-done, f32[128]{0:T(128)S(1)} %convert_element_type.88), kind=kOutput, calls=%fused_computation.19 | convolution fusion | flops 2160099328 | bytes 33620480 | tf_op jit(solution)/shard_map/dot_general | solution.py:29
  (1 shorter events, 0.0 us)
Async XLA Ops:
  7.2 126.9 %all-gather.7.cloned.1.call-start = ((), (), s32[]{:S(2)}) async-start(), calls=%async_computation | async-start | bytes 8421376 | tf_op jit(solution)/shard_map/all_gather | solution.py:24
  7.9 244.5 %all-gather.11.cloned.1.call-start = ((), (), s32[]{:S(2)}) async-start(), calls=%async_computation.2 | async-start | bytes 8421376 | tf_op jit(solution)/shard_map/all_gather | solution.py:30
  8.6 362.3 %all-gather.13.cloned.1.call-start = ((), (), s32[]{:S(2)}) async-start(), calls=%async_computation.3 | async-start | bytes 8421376 | tf_op jit(solution)/shard_map/all_gather | solution.py:31
  9.4 479.9 %all-gather.9.cloned.1.call-start = ((), (), s32[]{:S(2)}) async-start(), calls=%async_computation.1 | async-start | bytes 8421376 | tf_op jit(solution)/shard_map/all_gather | solution.py:25
  126.7 125.7 %copy-start.1 = (bf16[128,128]{1,0:T(8,128)(2,1)S(1)}, bf16[128,128]{1,0:T(8,128)(2,1)}, u32[]{:S(2)}) copy-start(bf16[128,128]{1,0:T(8,128)(2,1)} %param.7) | copy-start | bytes 98308
  268.9 113.2 %copy-start.2 = (bf16[128,128]{1,0:T(8,128)(2,1)S(1)}, bf16[128,128]{1,0:T(8,128)(2,1)}, u32[]{:S(2)}) copy-start(bf16[128,128]{1,0:T(8,128)(2,1)} %param.8) | copy-start | bytes 98308
  382.1 107.2 %copy-start = (bf16[128,128]{1,0:T(8,128)(2,1)S(1)}, bf16[128,128]{1,0:T(8,128)(2,1)}, u32[]{:S(2)}) copy-start(bf16[128,128]{1,0:T(8,128)(2,1)} %param.10) | copy-start | bytes 98308
Sparse Core Ops, SparseCore 0:
  11.6 122.4 all-gather.6
  137.7 114.7 all-gather.10
  256.0 114.8 all-gather.12
  374.4 114.8 all-gather.8
where the time goes:
time: 510 us; the launch traced here: 509 us
  waiting for transfers between devices  305 us (60%)
  blocking collectives  115 us (23%)
  matrix products  73.5 us (14%)
  between operations  13.8 us (3%)
    all_gather x1, waiting for transfers between devices, on_device(): query_piece = lax.all_gather(query_rows, 'ctx', axis=0, tiled=True)  107 us
    all_gather x1, waiting for transfers between devices, on_device(): grad_piece = lax.all_gather(grad_out, 'ctx', axis=0, tiled=True)  102 us
    all_gather x1, waiting for transfers between devices, on_device(): value_piece = lax.all_gather(value_rows, 'ctx', axis=0, tiled=True)  86.7 us
    all_gather x1, blocking collectives, on_device(): lse_piece = lax.all_gather(saved_lse, 'ctx', axis=0, tiled=True)  61.1 us
    all_gather x1, blocking collectives, on_device(): delta_piece = lax.all_gather(row_delta, 'ctx', axis=0, tiled=True)  53.8 us
    dot_general x2, matrix products, score_grads(): jnp.dot(query_part, keys.T, preferred_element_type=jnp.float32) * factor  28.2 us
    dot_general x1, matrix products, on_device(): jnp.dot(grad_score.T, query_piece, preferred_element_type=jnp.float32)  20.5 us
    dot_general x1, matrix products, on_device(): jnp.dot(grad_score, key_piece, preferred_element_type=jnp.float32)  13.5 us
  transfers between devices with their start and end apart: 4, of which 4 were waited for; matrix products, arithmetic and copies ran while one was open for 12% of the time, Pallas kernels for 0%

commit v1 on v0

v1 whole, which is shorter than its diff:
```python
import math

import jax
import jax.numpy as jnp
from jax import lax
from jax.experimental import pallas as pl
from jax.experimental.pallas import tpu as pltpu
from jax.sharding import PartitionSpec as P

HEAD = 128
TOK = 128
AUX = 16
NX, NY, NZ = 4, 4, 8
SIDE = NX * NY * TOK
TILE = 512
FACTOR = HEAD**-0.5
LOG2E = math.log2(math.e)
F32, BF16 = jnp.float32, jnp.bfloat16
MESH = pl.DeviceIdType.MESH

Z_ORDER = (0, 4, 3, 5, 2, 6, 1, 7)
XY = tuple((dx, dy) for dy in range(NY) for dx in range(NX) if dx or dy)


def dot(a, b):
    return jnp.dot(a, b, preferred_element_type=F32)


def dot_nt(a, b):
    return lax.dot_general(a, b, (((1,), (1,)), ((), ())), preferred_element_type=F32)


def rows(block):
    return pl.ds(block * TOK, TOK)


def kernel(
    q_ref, k_ref, v_ref, so_ref, do_ref, lse_ref, out_ref,
    q_land, d_land, kv, so_buf, lse_buf, q_all, d_all, kt, lse_all, delta_all,
    dq_acc, dk_acc, dv_acc, sib_out, sib_in, z_out, z_in, dq_out, dq_in,
    local_sem, send_sem, q_sem, d_sem, kv_sem, rel_sem, sib_sem, z_sem, dq_sem,
):
    me = lax.axis_index("ctx")
    core, x = lax.rem(me, 2), lax.rem(me // 2, NX)
    y, z = lax.rem(me // (2 * NX), NY), me // (2 * NX * NY)

    def device(core, x, y, z):
        return ((z * NY + y) * NX + x) * 2 + core

    def at_xy(dx, dy):
        return device(core, lax.rem(x + dx, NX), lax.rem(y + dy, NY), z)

    def at_z(dz):
        return device(core, x, y, lax.rem(z + dz, NZ))

    sibling = device(1 - core, x, y, z)

    fetch = [
        pltpu.make_async_copy(src, dst, local_sem.at[i])
        for i, (src, dst) in enumerate((
            (so_ref, so_buf),
            (do_ref, d_land.at[0, pl.ds(0, TOK)]),
            (q_ref, q_land.at[0, pl.ds(0, TOK)]),
            (lse_ref, lse_buf),
            (k_ref, kv.at[0, rows(0)]),
            (v_ref, kv.at[1, rows(0)]),
        ))
    ]
    for copy in fetch:
        copy.start()

    barrier = pltpu.get_barrier_semaphore()
    partners = [sibling]
    partners += [at_xy(dx, dy) for dx, dy in XY]
    partners += [at_z(d) for d in range(1, NZ)]
    for p in partners:
        pl.semaphore_signal(barrier, 1, device_id=(p,), device_id_type=MESH)

    for copy in fetch:
        copy.wait()
    lse_row = jnp.reshape(lse_buf[...].astype(F32), (1, TOK)).astype(BF16)
    q_land[0, pl.ds(TOK, AUX)] = jnp.broadcast_to(lse_row, (AUX, TOK))
    product = d_land[0, pl.ds(0, TOK)].astype(F32) * so_buf[...].astype(F32)
    delta_row = jnp.sum(product.T, axis=0, keepdims=True).astype(BF16)
    d_land[0, pl.ds(TOK, AUX)] = jnp.broadcast_to(delta_row, (AUX, TOK))

    pl.semaphore_wait(barrier, len(partners))

    sends = []

    def send(src, dst, recv_sem, target):
        copy = pltpu.make_async_remote_copy(
            src_ref=src, dst_ref=dst, send_sem=send_sem.at[len(sends)], recv_sem=recv_sem,
            device_id=(target,), device_id_type=MESH,
        )
        copy.start()
        sends.append(copy)

    def arrived(dst, recv_sem):
        pltpu.make_async_remote_copy(
            src_ref=dst, dst_ref=dst, send_sem=send_sem.at[0], recv_sem=recv_sem,
            device_id=(sibling,), device_id_type=MESH,
        ).wait_recv()

    def kv_at(p, other):
        return kv.at[:, rows(2 * p + other)]

    send(kv_at(0, 0), kv_at(0, 1), rel_sem.at[0], sibling)
    near = (1, 3, 2)
    for d in near:
        send(q_land.at[0], q_land.at[d], q_sem.at[d], at_xy(d, 0))
        send(d_land.at[0], d_land.at[d * NX], d_sem.at[d * NX], at_xy(0, d))
    for p, d in enumerate(Z_ORDER):
        if d:
            send(kv_at(0, 0), kv_at(p, 0), kv_sem.at[p], at_z(d))
    for d in near:
        send(q_land.at[0], q_land.at[d * NX], q_sem.at[d * NX], at_xy(0, d))
        send(d_land.at[0], d_land.at[d], d_sem.at[d], at_xy(d, 0))
    for e in near:
        arrived(q_land.at[e], q_sem.at[e])
        for d in near:
            s = d * NX + e
            send(q_land.at[e], q_land.at[s], q_sem.at[s], at_xy(0, d))
        arrived(d_land.at[e * NX], d_sem.at[e * NX])
        for d in near:
            s = e * NX + d
            send(d_land.at[e * NX], d_land.at[s], d_sem.at[s], at_xy(d, 0))

    for s in range(NX * NY):
        if s >= NX:
            arrived(q_land.at[s], q_sem.at[s])
        if s % NX:
            arrived(d_land.at[s], d_sem.at[s])
        q_all[rows(s)] = q_land[s, pl.ds(0, TOK)]
        d_all[rows(s)] = d_land[s, pl.ds(0, TOK)]
        lse_all[:, rows(s)] = q_land[s, pl.ds(TOK, AUX)][0:1].astype(F32) * LOG2E
        delta_all[:, rows(s)] = d_land[s, pl.ds(TOK, AUX)][0:1].astype(F32)

    dq_acc[...] = jnp.zeros_like(dq_acc)
    dk_acc[...] = jnp.zeros_like(dk_acc)
    dv_acc[...] = jnp.zeros_like(dv_acc)

    def tile(ks, qs):
        scores = dot_nt(kv[0, ks], q_all[qs])
        probs = dot_nt(kv[1, ks], d_all[qs])
        weights = jnp.exp2(scores * (FACTOR * LOG2E) - lse_all[:, qs])
        grads = (weights * (probs - delta_all[:, qs])).astype(BF16)
        dv_acc[ks] += dot(weights.astype(BF16), d_all[qs])
        dk_acc[ks] += dot(grads, q_all[qs])
        dq_acc[:, qs] += dot(kt[:, ks], grads)

    def to_sibling(g):
        for p in (2 * g, 2 * g + 1):
            r = rows(2 * p + 1)
            sib_out[p, 0] = dk_acc[r].astype(BF16)
            sib_out[p, 1] = dv_acc[r].astype(BF16)
            send(sib_out.at[p], sib_in.at[p], sib_sem.at[p], sibling)

    def to_owner(g):
        for p in (2 * g, 2 * g + 1):
            r = rows(2 * p)
            arrived(sib_in.at[p], sib_sem.at[p])
            dk = dk_acc[r] + sib_in[p, 0].astype(F32)
            dv = dv_acc[r] + sib_in[p, 1].astype(F32)
            if p == 0:
                dk_acc[r], dv_acc[r] = dk, dv
            else:
                z_out[p, 0], z_out[p, 1] = dk.astype(BF16), dv.astype(BF16)
                send(z_out.at[p], z_in.at[p], z_sem.at[p], at_z(NZ - Z_ORDER[p]))

    for g in range(4):
        for p in (2 * g, 2 * g + 1):
            if p:
                arrived(kv_at(p, 0), kv_sem.at[p])
                send(kv_at(p, 0), kv_at(p, 1), rel_sem.at[p], sibling)
        for p in (2 * g, 2 * g + 1):
            arrived(kv_at(p, 1), rel_sem.at[p])
        ks = pl.ds(g * TILE, TILE)
        kt[:, ks] = kv[0, ks].T

        def step(i, carry):
            tile(ks, pl.ds(pl.multiple_of(i * TILE, TILE), TILE))
            return carry

        lax.fori_loop(0, SIDE // TILE, step, 0)
        to_sibling(g)
        if g:
            to_owner(g - 1)
    to_owner(3)

    for dx, dy in XY:
        s = dy * NX + dx
        dq_out[s] = dq_acc[:, rows(s)].T.astype(BF16)
        send(dq_out.at[s], dq_in.at[s], dq_sem.at[s], at_xy(NX - dx, NY - dy))

    dk, dv = dk_acc[rows(0)], dv_acc[rows(0)]
    for p in range(1, NZ):
        arrived(z_in.at[p], z_sem.at[p])
        dk += z_in[p, 0].astype(F32)
        dv += z_in[p, 1].astype(F32)
    out_ref[1] = (dk * FACTOR).astype(BF16)
    out_ref[2] = dv.astype(BF16)
    dq = dq_acc[:, rows(0)].T
    for s in range(1, NX * NY):
        arrived(dq_in.at[s], dq_sem.at[s])
        dq += dq_in[s].astype(F32)
    out_ref[0] = (dq * FACTOR).astype(BF16)
    for copy in sends:
        copy.wait_send()


def on_device(*args):
    vmem, dma = pltpu.VMEM, pltpu.SemaphoreType.DMA
    blocks = NX * NY
    out = pl.pallas_call(
        kernel,
        out_shape=jax.ShapeDtypeStruct((3, TOK, HEAD), BF16),
        in_specs=[pl.BlockSpec(memory_space=pltpu.HBM)] * 6,
        out_specs=pl.BlockSpec(memory_space=pltpu.VMEM),
        scratch_shapes=[
            vmem((blocks, TOK + AUX, HEAD), BF16),
            vmem((blocks, TOK + AUX, HEAD), BF16),
            vmem((2, SIDE, HEAD), BF16),
            vmem((TOK, HEAD), BF16),
            vmem((TOK,), BF16),
            vmem((SIDE, HEAD), BF16),
            vmem((SIDE, HEAD), BF16),
            vmem((HEAD, SIDE), BF16),
            vmem((1, SIDE), F32),
            vmem((1, SIDE), F32),
            vmem((HEAD, SIDE), F32),
            vmem((SIDE, HEAD), F32),
            vmem((SIDE, HEAD), F32),
            vmem((NZ, 2, TOK, HEAD), BF16),
            vmem((NZ, 2, TOK, HEAD), BF16),
            vmem((NZ, 2, TOK, HEAD), BF16),
            vmem((NZ, 2, TOK, HEAD), BF16),
            vmem((blocks, TOK, HEAD), BF16),
            vmem((blocks, TOK, HEAD), BF16),
            dma((6,)),
            dma((76,)),
            dma((blocks,)),
            dma((blocks,)),
            dma((NZ,)),
            dma((NZ,)),
            dma((NZ,)),
            dma((NZ,)),
            dma((blocks,)),
        ],
        compiler_params=pltpu.CompilerParams(
            collective_id=0, has_side_effects=True, vmem_limit_bytes=62 << 20
        ),
        name="attention_backward",
    )(*args)
    return out[0], out[1], out[2]


def solution(mesh):
    tokens = P("ctx", None)
    return jax.shard_map(
        on_device,
        mesh=mesh,
        in_specs=(tokens,) * 5 + (P("ctx"),),
        out_specs=(tokens,) * 3,
        check_vma=False,
    )
```

time: 510 us -> 54.2 us (0.11)
  waiting for transfers between devices: 305 us -> 0 us
  blocking collectives: 115 us -> 0 us
  matrix products: 73.5 us -> 0 us
  Pallas kernels: 0 us -> 51.9 us
  between operations: 13.8 us -> 0.64 us
    all_gather x4 -> x0, waiting for transfers between devices: 303 us -> none  [the longest x1 107 us: on_device(): query_piece = lax.all_gather(query_rows, 'ctx', axis=0, tiled=True)]
    all_gather x2 -> x0, blocking collectives: 115 us -> none  [the longest x1 61.1 us: on_device(): lse_piece = lax.all_gather(saved_lse, 'ctx', axis=0, tiled=True)]
    dot_general x5 -> x0, matrix products: 73.5 us -> none  [the longest x2 28.2 us: score_grads(): jnp.dot(query_part, keys.T, preferred_element_type=jnp.float32) * factor]
    pallas_call x0 -> x1, Pallas kernels: none -> 51.9 us  [on_device(): pl.pallas_call(kernel, out_shape=jax.ShapeDtypeStruct((3, TOK, HEAD), BF1...]
  transfers between devices with their start and end apart: 4 -> 0, of which waited for: 4 -> 0; matrix products, arithmetic and copies ran while one was open for 12% -> 0% of each run, Pallas kernels for 0% -> 0%
where the time goes in v1:
time: 54.2 us; the launch traced here: 54 us
  Pallas kernels  51.9 us (96%)
  local copies, waits for them, and re-layouts  1.43 us (3%)
  between operations  0.64 us (1%)
    pallas_call x1, Pallas kernels, on_device(): pl.pallas_call(kernel, out_shape=jax.ShapeDtypeStruct((3, TOK, HEAD), BF1...  51.9 us
    squeeze x1, local copies, waits for them, and re-layouts, on_device(): return (out[0], out[1], out[2])  1.43 us

profile of v1, /device:TPU:1, one launch (start us, length us, event | category | flops | bytes accessed | tf_op | source)
XLA Modules:
  0.0 54.0 jit_solution(14711873918522222715)
XLA Ops:
  0.6 51.9 %attention_backward.1 = bf16[3,128,128]{2,1,0:T(8,128)(2,1)} custom-call(bf16[128,128]{1,0:T(8,128)(2,1)} %q_ref.1, bf16[128,128]{1,0:T(8,128)(2,1)} %k_ref.1, bf16[128,128]{1,0:T(8,128)(2,1)} %v_ref.1, bf16[128,128]{1,0:T(8,128)(2,1)} %so_ref.1, bf16[128,128]{1,0:T(8,128)(2,1)} %do_ref.1, bf16[128]{0:T(256)(128)(2,1)} %lse_ref.1), custom_call_target="tpu_custom_call" | custom-call | tf_op jit(solution)/shard_map/attention_backward/pallas_call | solution.py:215
  52.6 1.4 %slice_bitcast_fusion = (bf16[128,128]{1,0:T(8,128)(2,1)}, bf16[128,128]{1,0:T(8,128)(2,1)}, bf16[128,128]{1,0:T(8,128)(2,1)}) fusion(bf16[3,128,128]{2,1,0:T(8,128)(2,1)} %attention_backward.1), kind=kLoop, calls=%fused_computation | loop fusion | bytes 196608 | tf_op jit(solution)/shard_map/squeeze | solution.py:255

commit v2 on v1

v2 whole, which is shorter than its diff:
```python
import math

import jax
import jax.numpy as jnp
from jax import lax
from jax.experimental import pallas as pl
from jax.experimental.pallas import tpu as pltpu
from jax.sharding import PartitionSpec as P

HEAD = 128
TOK = 128
AUX = 16
NX, NY, NZ = 4, 4, 8
SIDE = NX * NY * TOK
TILE = 512
FACTOR = HEAD**-0.5
LOG2E = math.log2(math.e)
F32, BF16 = jnp.float32, jnp.bfloat16
MESH = pl.DeviceIdType.MESH

Z_ORDER = (0, 1, 7, 2, 6, 3, 5, 4)
AT = {d: p for p, d in enumerate(Z_ORDER)}
A, B, C, D = range(4)
NEAR = (1, 3, 2)


def dot(a, b):
    return jnp.dot(a, b, preferred_element_type=F32)


def dot_nt(a, b):
    return lax.dot_general(a, b, (((1,), (1,)), ((), ())), preferred_element_type=F32)


def rows(block):
    return pl.ds(block * TOK, TOK)


def kernel(
    q_ref, k_ref, v_ref, so_ref, do_ref, lse_ref, out_ref,
    q_land, d_land, kv, so_buf, lse_buf, q_all, d_all, kt, lse_all, delta_all,
    dq_acc, dk_acc, dv_acc, sib_out, sib_in, z_out, z_in, dq_out, dq_in,
    local_sem, send_sem, q_sem, d_sem, kv_sem, rel_sem, sib_sem, z_sem, dq_sem,
):
    me = lax.axis_index("ctx")
    core, x = lax.rem(me, 2), lax.rem(me // 2, NX)
    y, z = lax.rem(me // (2 * NX), NY), me // (2 * NX * NY)

    def device(core, x, y, z):
        return ((z * NY + y) * NX + x) * 2 + core

    def at_xy(dx, dy):
        return device(core, lax.rem(x + dx, NX), lax.rem(y + dy, NY), z)

    def at_z(dz):
        return device(core, x, y, lax.rem(z + dz, NZ))

    sibling = device(1 - core, x, y, z)

    barrier = pltpu.get_barrier_semaphore()
    partners = [sibling]
    partners += [at_xy(d, 0) for d in NEAR] + [at_xy(0, d) for d in NEAR]
    partners += [at_z(d) for d in (1, 7, 2, 6)]
    for p in partners:
        pl.semaphore_signal(barrier, 1, device_id=(p,), device_id_type=MESH)

    fetch = [
        pltpu.make_async_copy(src, dst, local_sem.at[i])
        for i, (src, dst) in enumerate((
            (so_ref, so_buf),
            (do_ref, d_land.at[0, pl.ds(0, TOK)]),
            (q_ref, q_land.at[0, pl.ds(0, TOK)]),
            (lse_ref, lse_buf),
            (k_ref, kv.at[0, rows(0)]),
            (v_ref, kv.at[1, rows(0)]),
        ))
    ]
    for copy in fetch:
        copy.start()
    for copy in fetch:
        copy.wait()
    lse_row = jnp.reshape(lse_buf[...].astype(F32), (1, TOK)).astype(BF16)
    q_land[0, pl.ds(TOK, AUX)] = jnp.broadcast_to(lse_row, (AUX, TOK))
    product = d_land[0, pl.ds(0, TOK)].astype(F32) * so_buf[...].astype(F32)
    delta_row = jnp.sum(product.T, axis=0, keepdims=True).astype(BF16)
    d_land[0, pl.ds(TOK, AUX)] = jnp.broadcast_to(delta_row, (AUX, TOK))
    dq_acc[...] = jnp.zeros_like(dq_acc)
    dk_acc[...] = jnp.zeros_like(dk_acc)
    dv_acc[...] = jnp.zeros_like(dv_acc)
    pl.semaphore_wait(barrier, len(partners))

    def send(src, dst, kind, recv_sem, target):
        pltpu.make_async_remote_copy(
            src_ref=src, dst_ref=dst, send_sem=send_sem.at[kind], recv_sem=recv_sem,
            device_id=(target,), device_id_type=MESH,
        ).start()

    def of(ref, kind, recv_sem):
        return pltpu.make_async_remote_copy(
            src_ref=ref, dst_ref=ref, send_sem=send_sem.at[kind], recv_sem=recv_sem,
            device_id=(sibling,), device_id_type=MESH,
        )

    def arrived(dst, recv_sem):
        of(dst, 0, recv_sem).wait_recv()

    def kv_at(p, other):
        return kv.at[:, rows(2 * p + other)]

    def half(h, p):
        return kv.at[h, rows(2 * p)]

    def send_kv(src, d, dz):
        send(src, kv_at(AT[d], 0), 2, kv_sem.at[AT[d]], at_z(dz))

    def to_other_core(d):
        p = AT[d]
        send(kv_at(p, 0), kv_at(p, 1), 2, rel_sem.at[p], sibling)

    def send_q(src, dx, dy, sem, hx, hy):
        send(q_land.at[src], q_land.at[dy * NX + dx], 0, q_sem.at[sem], at_xy(hx, hy))

    def send_d(src, dx, dy, sem, hx, hy):
        send(d_land.at[src], d_land.at[dy * NX + dx], 1, d_sem.at[sem], at_xy(hx, hy))

    to_other_core(0)
    for d in NEAR:
        send_q(0, d, 0, d, d, 0)
        send_d(0, 0, d, 3 + d, 0, d)
    for d in (2, 6, 1, 7):
        send_kv(kv_at(0, 0), d, d)
    for d in NEAR:
        send_d(0, d, 0, d, d, 0)
        send_q(0, 0, d, 3 + d, 0, d)
    for e in NEAR:
        arrived(q_land.at[e], q_sem.at[e])
        for d in NEAR:
            send_q(e, e, d, 6 + d, 0, d)
        arrived(d_land.at[e * NX], d_sem.at[3 + e])
        for d in NEAR:
            send_d(e * NX, d, e, 6 + e, d, 0)
    for d, far, hop, mid, h in ((2, 3, 1, 2, 0), (6, 5, 7, 6, 1)):
        arrived(kv_at(AT[d], 0), kv_sem.at[AT[d]])
        send_kv(kv_at(AT[d], 0), far, hop)
        send(half(h, AT[d]), half(h, AT[4]), 2, kv_sem.at[AT[4] if h == 0 else 0], at_z(mid))
        to_other_core(d)
    for d in (1, 7):
        arrived(kv_at(AT[d], 0), kv_sem.at[AT[d]])
        to_other_core(d)

    def land(dy):
        for e in NEAR:
            if dy == 0:
                arrived(d_land.at[e], d_sem.at[e])
        if dy:
            arrived(q_land.at[dy * NX], q_sem.at[3 + dy])
            arrived(q_land.at[pl.ds(dy * NX + 1, 3)], q_sem.at[6 + dy])
            arrived(d_land.at[pl.ds(dy * NX + 1, 3)], d_sem.at[6 + dy])
        for s in range(dy * NX, dy * NX + NX):
            q_all[rows(s)] = q_land[s, pl.ds(0, TOK)]
            d_all[rows(s)] = d_land[s, pl.ds(0, TOK)]
            lse_all[:, rows(s)] = q_land[s, pl.ds(TOK, AUX)][0:1].astype(F32) * LOG2E
            delta_all[:, rows(s)] = d_land[s, pl.ds(TOK, AUX)][0:1].astype(F32)

    def keys_ready(g):
        for p in (2 * g, 2 * g + 1):
            arrived(kv_at(p, 1), rel_sem.at[p])
        ks = pl.ds(g * TILE, TILE)
        kt[:, ks] = kv[0, ks].T

    def tile(g, dy):
        start = g * TILE if isinstance(g, int) else pl.multiple_of(g * TILE, TILE)
        ks = pl.ds(start, TILE)
        start = dy * TILE if isinstance(dy, int) else pl.multiple_of(dy * TILE, TILE)
        qs = pl.ds(start, TILE)
        scores = dot_nt(kv[0, ks], q_all[qs])
        probs = dot_nt(kv[1, ks], d_all[qs])
        weights = jnp.exp2(scores * (FACTOR * LOG2E) - lse_all[:, qs])
        grads = (weights * (probs - delta_all[:, qs])).astype(BF16)
        dv_acc[ks] += dot(weights.astype(BF16), d_all[qs])
        dk_acc[ks] += dot(grads, q_all[qs])
        dq_acc[:, qs] += dot(kt[:, ks], grads)

    def over_keys(n, dy):
        lax.fori_loop(0, n, lambda g, c: (tile(g, dy), c)[1], 0)

    def over_queries(g):
        lax.fori_loop(0, NY, lambda i, c: (tile(g, i), c)[1], 0)

    def to_sibling(g):
        for p in (2 * g, 2 * g + 1):
            r = rows(2 * p + 1)
            sib_out[p, 0] = dk_acc[r].astype(BF16)
            sib_out[p, 1] = dv_acc[r].astype(BF16)
            send(sib_out.at[p], sib_in.at[p], 3, sib_sem.at[p], sibling)

    def to_owner(g):
        for p in (2 * g, 2 * g + 1):
            r = rows(2 * p)
            arrived(sib_in.at[p], sib_sem.at[p])
            dk = dk_acc[r] + sib_in[p, 0].astype(F32)
            dv = dv_acc[r] + sib_in[p, 1].astype(F32)
            if p == 0:
                dk_acc[r], dv_acc[r] = dk, dv
            else:
                z_out[p, 0], z_out[p, 1] = dk.astype(BF16), dv.astype(BF16)
                send(z_out.at[p], z_in.at[p], 4, z_sem.at[p], at_z(NZ - Z_ORDER[p]))

    def queries_done(dy):
        for dx in range(NX):
            s = dy * NX + dx
            if s:
                dq_out[s] = dq_acc[:, rows(s)].T.astype(BF16)
                send(dq_out.at[s], dq_in.at[s], 5, dq_sem.at[s], at_xy((NX - dx) % NX, (NY - dy) % NY))

    land(0)
    keys_ready(A)
    keys_ready(B)
    over_keys(2, 0)
    land(1)
    over_keys(2, 1)
    land(3)
    over_keys(2, 3)
    for d in (5, 3):
        arrived(kv_at(AT[d], 0), kv_sem.at[AT[d]])
        to_other_core(d)
    arrived(half(0, AT[4]), kv_sem.at[AT[4]])
    arrived(half(1, AT[4]), kv_sem.at[0])
    to_other_core(4)
    land(2)
    tile(B, 2)
    to_sibling(B)
    keys_ready(D)
    over_queries(D)
    to_sibling(D)
    to_owner(B)
    keys_ready(C)
    tile(C, 0)
    to_owner(D)
    queries_done(0)
    tile(C, 1)
    queries_done(1)
    tile(C, 3)
    queries_done(3)
    tile(C, 2)
    to_sibling(C)
    tile(A, 2)
    to_sibling(A)
    queries_done(2)
    to_owner(C)
    to_owner(A)
    dq = dq_acc[:, rows(0)].T
    for dy in (0, 1, 3, 2):
        for s in range(dy * NX, dy * NX + NX):
            if s:
                arrived(dq_in.at[s], dq_sem.at[s])
                dq += dq_in[s].astype(F32)
    out_ref[0] = (dq * FACTOR).astype(BF16)
    dk, dv = dk_acc[rows(0)], dv_acc[rows(0)]
    for p in (2, 3, 6, 7, 4, 5, 1):
        arrived(z_in.at[p], z_sem.at[p])
        dk += z_in[p, 0].astype(F32)
        dv += z_in[p, 1].astype(F32)
    out_ref[1] = (dk * FACTOR).astype(BF16)
    out_ref[2] = dv.astype(BF16)
    of(q_land.at[pl.ds(1, 15)], 0, q_sem.at[0]).wait_send()
    of(d_land.at[pl.ds(1, 15)], 1, q_sem.at[0]).wait_send()
    of(kv.at[:, pl.ds(0, 15 * TOK)], 2, q_sem.at[0]).wait_send()
    of(sib_out, 3, q_sem.at[0]).wait_send()
    of(z_out.at[pl.ds(1, 7)], 4, q_sem.at[0]).wait_send()
    of(dq_out.at[pl.ds(1, 15)], 5, q_sem.at[0]).wait_send()


def on_device(*args):
    vmem, dma = pltpu.VMEM, pltpu.SemaphoreType.DMA
    blocks = NX * NY
    out = pl.pallas_call(
        kernel,
        out_shape=jax.ShapeDtypeStruct((3, TOK, HEAD), BF16),
        in_specs=[pl.BlockSpec(memory_space=pltpu.HBM)] * 6,
        out_specs=pl.BlockSpec(memory_space=pltpu.VMEM),
        scratch_shapes=[
            vmem((blocks, TOK + AUX, HEAD), BF16),
            vmem((blocks, TOK + AUX, HEAD), BF16),
            vmem((2, SIDE, HEAD), BF16),
            vmem((TOK, HEAD), BF16),
            vmem((TOK,), BF16),
            vmem((SIDE, HEAD), BF16),
            vmem((SIDE, HEAD), BF16),
            vmem((HEAD, SIDE), BF16),
            vmem((1, SIDE), F32),
            vmem((1, SIDE), F32),
            vmem((HEAD, SIDE), F32),
            vmem((SIDE, HEAD), F32),
            vmem((SIDE, HEAD), F32),
            vmem((NZ, 2, TOK, HEAD), BF16),
            vmem((NZ, 2, TOK, HEAD), BF16),
            vmem((NZ, 2, TOK, HEAD), BF16),
            vmem((NZ, 2, TOK, HEAD), BF16),
            vmem((blocks, TOK, HEAD), BF16),
            vmem((blocks, TOK, HEAD), BF16),
            dma((6,)),
            dma((6,)),
            dma((10,)),
            dma((10,)),
            dma((NZ,)),
            dma((NZ,)),
            dma((NZ,)),
            dma((NZ,)),
            dma((blocks,)),
        ],
        compiler_params=pltpu.CompilerParams(
            collective_id=0, has_side_effects=True, vmem_limit_bytes=62 << 20
        ),
        name="attention_backward",
    )(*args)
    return out[0], out[1], out[2]


def solution(mesh):
    tokens = P("ctx", None)
    return jax.shard_map(
        on_device,
        mesh=mesh,
        in_specs=(tokens,) * 5 + (P("ctx"),),
        out_specs=(tokens,) * 3,
        check_vma=False,
    )
```

time: 54.2 us -> 44.5 us (0.82)
  Pallas kernels: 51.9 us -> 42.3 us
    pallas_call x1, Pallas kernels: 51.9 us -> 42.3 us  [on_device(): pl.pallas_call(kernel, out_shape=jax.ShapeDtypeStruct((3, TOK, HEAD), BF1...]
where the time goes in v2:
time: 44.5 us; the launch traced here: 44.3 us
  Pallas kernels  42.3 us (95%)
  local copies, waits for them, and re-layouts  1.43 us (3%)
  between operations  0.64 us (1%)
    pallas_call x1, Pallas kernels, on_device(): pl.pallas_call(kernel, out_shape=jax.ShapeDtypeStruct((3, TOK, HEAD), BF1...  42.3 us
    squeeze x1, local copies, waits for them, and re-layouts, on_device(): return (out[0], out[1], out[2])  1.43 us

profile of v2, /device:TPU:1, one launch (start us, length us, event | category | flops | bytes accessed | tf_op | source)
XLA Modules:
  0.0 44.3 jit_solution(11334278684543960879)
XLA Ops:
  0.6 42.3 %attention_backward.1 = bf16[3,128,128]{2,1,0:T(8,128)(2,1)} custom-call(bf16[128,128]{1,0:T(8,128)(2,1)} %q_ref.1, bf16[128,128]{1,0:T(8,128)(2,1)} %k_ref.1, bf16[128,128]{1,0:T(8,128)(2,1)} %v_ref.1, bf16[128,128]{1,0:T(8,128)(2,1)} %so_ref.1, bf16[128,128]{1,0:T(8,128)(2,1)} %do_ref.1, bf16[128]{0:T(256)(128)(2,1)} %lse_ref.1), custom_call_target="tpu_custom_call" | custom-call | tf_op jit(solution)/shard_map/attention_backward/pallas_call | solution.py:277
  42.9 1.4 %slice_bitcast_fusion = (bf16[128,128]{1,0:T(8,128)(2,1)}, bf16[128,128]{1,0:T(8,128)(2,1)}, bf16[128,128]{1,0:T(8,128)(2,1)}) fusion(bf16[3,128,128]{2,1,0:T(8,128)(2,1)} %attention_backward.1), kind=kLoop, calls=%fused_computation | loop fusion | bytes 196608 | tf_op jit(solution)/shard_map/squeeze | solution.py:317

commit v3 on v2

v3 whole, which is shorter than its diff:
```python
import math

import jax
import jax.numpy as jnp
from jax import lax
from jax.experimental import pallas as pl
from jax.experimental.pallas import tpu as pltpu
from jax.sharding import PartitionSpec as P

HEAD = 128
TOK = 128
AUX = 16
NX, NY, NZ = 4, 4, 8
KEYS = NZ * TOK
HALF = NX * TOK
ROW = 2 * HALF
QUERIES = NY * ROW
PAIR = 2 * TOK
FACTOR = HEAD**-0.5
LOG2E = math.log2(math.e)
F32, BF16 = jnp.float32, jnp.bfloat16
MESH = pl.DeviceIdType.MESH

Z_ORDER = (0, 1, 2, 6, 4, 7, 3, 5)
AT = {d: p for p, d in enumerate(Z_ORDER)}
A, B, C, D = range(4)
NEAR = (1, 3, 2)
ROW_AT = (0, 3, 2, 1)


def dot(a, b):
    return jnp.dot(a, b, preferred_element_type=F32)


def dot_nt(a, b):
    return lax.dot_general(a, b, (((1,), (1,)), ((), ())), preferred_element_type=F32)


def rows(block):
    return pl.ds(block * TOK, TOK)


def kernel(
    q_ref, k_ref, v_ref, so_ref, do_ref, lse_ref, out_ref,
    d_land, kv, so_buf, lse_buf, q_all, d_all, kt, lse_all, delta_all,
    dq_acc, dk_acc, dv_acc, z_out, z_in, sib_out, sib_in, dq_out, dq_in,
    local_sem, send_sem, q_sem, d_sem, kv_sem, sib_sem, z_sem, dq_sem,
):
    me = lax.axis_index("ctx")
    core, x = lax.rem(me, 2), lax.rem(me // 2, NX)
    y, z = lax.rem(me // (2 * NX), NY), me // (2 * NX * NY)

    def device(core, x, y, z):
        return ((z * NY + y) * NX + x) * 2 + core

    def at_xy(dx, dy):
        return device(core, lax.rem(x + dx, NX), lax.rem(y + dy, NY), z)

    def at_z(dz):
        return device(core, x, y, lax.rem(z + dz, NZ))

    sibling = device(1 - core, x, y, z)

    barrier = pltpu.get_barrier_semaphore()
    partners = [sibling]
    partners += [at_xy(d, 0) for d in NEAR] + [at_xy(0, d) for d in NEAR]
    partners += [at_z(d) for d in (1, 7, 2, 6)]
    for p in partners:
        pl.semaphore_signal(barrier, 1, device_id=(p,), device_id_type=MESH)

    fetch = [
        pltpu.make_async_copy(src, dst, local_sem.at[i])
        for i, (src, dst) in enumerate((
            (q_ref, q_all.at[pl.ds(0, TOK)]),
            (lse_ref, lse_buf),
            (so_ref, so_buf),
            (do_ref, d_land.at[0, pl.ds(0, TOK)]),
            (k_ref, kv.at[0, rows(0)]),
            (v_ref, kv.at[1, rows(0)]),
        ))
    ]
    for copy in fetch:
        copy.start()
    pl.semaphore_wait(barrier, len(partners))

    def send(src, dst, kind, recv_sem, target):
        pltpu.make_async_remote_copy(
            src_ref=src, dst_ref=dst, send_sem=send_sem.at[kind], recv_sem=recv_sem,
            device_id=(target,), device_id_type=MESH,
        ).start()

    def of(ref, kind, recv_sem):
        return pltpu.make_async_remote_copy(
            src_ref=ref, dst_ref=ref, send_sem=send_sem.at[kind], recv_sem=recv_sem,
            device_id=(sibling,), device_id_type=MESH,
        )

    def arrived(dst, recv_sem):
        of(dst, 0, recv_sem).wait_recv()

    def kv_at(p):
        return kv.at[:, rows(p)]

    def send_kv(src, d, dz):
        send(src, kv_at(AT[d]), 2, kv_sem.at[AT[d]], at_z(dz))

    def queries(dx, dy, other=0, n=1):
        return q_all.at[pl.ds(ROW_AT[dy] * ROW + other * HALF + dx * TOK, n * TOK)]

    def send_q(src, dx, dy, sem, hx, hy):
        send(src, queries(dx, dy), 0, q_sem.at[sem], at_xy(hx, hy))

    def send_d(src, dx, dy, sem, hx, hy):
        send(d_land.at[src], d_land.at[dy * NX + dx], 1, d_sem.at[sem], at_xy(hx, hy))

    for d in (2, 6, 1, 7):
        for h, src in enumerate((k_ref, v_ref)):
            send(src, kv.at[h, rows(AT[d])], 2, kv_sem.at[AT[d]], at_z(d))
    for d in NEAR:
        send_q(q_ref, d, 0, d, d, 0)
    for i in (1, 2, 3):
        fetch[i].wait()
    product = d_land[0, pl.ds(0, TOK)].astype(F32) * so_buf[...].astype(F32)
    delta_row = jnp.sum(product.T, axis=0, keepdims=True)
    lse_row = jnp.reshape(lse_buf[...].astype(F32), (1, TOK))
    first = lax.broadcasted_iota(jnp.int32, (AUX, TOK), 0) == 0
    d_land[0, pl.ds(TOK, AUX)] = jnp.where(first, lse_row, delta_row).astype(BF16)
    for d in NEAR:
        send_d(0, 0, d, 3 + d, 0, d)
    for d in NEAR:
        send_d(0, d, 0, d, d, 0)
        send_q(q_ref, 0, d, 3 + d, 0, d)
    fetch[0].wait()
    fetch[4].wait()
    fetch[5].wait()
    dq_acc[...] = jnp.zeros_like(dq_acc)
    dk_acc[...] = jnp.zeros_like(dk_acc)
    dv_acc[...] = jnp.zeros_like(dv_acc)

    def row(dy, other):
        return pl.ds(other * NX * NY + dy * NX, NX)

    def take(dy, other):
        for s in range(NX):
            block = other * NX * NY + dy * NX + s
            to = pl.ds(ROW_AT[dy] * ROW + other * HALF + s * TOK, TOK)
            d_all[to] = d_land[block, pl.ds(0, TOK)]
            aux = d_land[block, pl.ds(TOK, AUX)].astype(F32)
            lse_all[:, to] = aux[0:1] * LOG2E
            delta_all[:, to] = aux[1:2]

    def land(dy):
        if dy:
            arrived(queries(0, dy), q_sem.at[3 + dy])
            arrived(queries(1, dy, 0, 3), q_sem.at[6 + dy])
            arrived(d_land.at[pl.ds(dy * NX + 1, 3)], d_sem.at[6 + dy])
        else:
            for e in NEAR:
                arrived(d_land.at[e], d_sem.at[e])
        send(queries(0, dy, 0, NX), queries(0, dy, 1, NX), 0, q_sem.at[10 + dy], sibling)
        send(d_land.at[row(dy, 0)], d_land.at[row(dy, 1)], 1, d_sem.at[10 + dy], sibling)
        take(dy, 0)

    def land_other(dy):
        arrived(queries(0, dy, 1, NX), q_sem.at[10 + dy])
        arrived(d_land.at[row(dy, 1)], d_sem.at[10 + dy])
        take(dy, 1)

    def keys_ready(g):
        for p in (2 * g, 2 * g + 1):
            if p:
                arrived(kv_at(p), kv_sem.at[p])
        ks = pl.ds(g * PAIR, PAIR)
        kt[:, ks] = kv[0, ks].T

    def tile(k0, kn, q0, qn):
        ks, qs = pl.ds(k0, kn), pl.ds(q0, qn)
        scores = dot_nt(kv[0, ks], q_all[qs])
        probs = dot_nt(kv[1, ks], d_all[qs])
        weights = jnp.exp2(scores * (FACTOR * LOG2E) - lse_all[:, qs])
        grads = (weights * (probs - delta_all[:, qs])).astype(BF16)
        dv_acc[ks] += dot(weights.astype(BF16), d_all[qs])
        dk_acc[ks] += dot(grads, q_all[qs])
        dq_acc[:, qs] += dot(kt[:, ks], grads)

    def near_tile(dy, other):
        tile(0, 2 * PAIR, ROW_AT[dy] * ROW + other * HALF, HALF)

    def far_tile(g, first, n):
        tile(g * PAIR, PAIR, first * ROW, n * ROW)

    def to_owner(g):
        for p in (2 * g, 2 * g + 1):
            if p:
                z_out[p, 0] = dk_acc[rows(p)].astype(BF16)
                z_out[p, 1] = dv_acc[rows(p)].astype(BF16)
                send(z_out.at[p], z_in.at[p], 3, z_sem.at[p], at_z(NZ - Z_ORDER[p]))

    def partial(dy, other, dx):
        return dq_acc[:, pl.ds(ROW_AT[dy] * ROW + other * HALF + dx * TOK, TOK)]

    def to_sibling(dy):
        for dx in range(NX):
            sib_out[dy * NX + dx] = partial(dy, 1, dx).astype(BF16)
        r = row(dy, 0)
        send(sib_out.at[r], sib_in.at[r], 4, sib_sem.at[dy], sibling)

    def queries_done(dy):
        r = row(dy, 0)
        arrived(sib_in.at[r], sib_sem.at[dy])
        for dx in (0, 1, 3, 2):
            s = dy * NX + dx
            if s:
                dq_out[s] = (partial(dy, 0, dx) + sib_in[s].astype(F32)).astype(BF16)
                send(dq_out.at[s], dq_in.at[s], 5, dq_sem.at[s], at_xy((NX - dx) % NX, (NY - dy) % NY))

    for e in NEAR:
        arrived(queries(e, 0), q_sem.at[e])
        for d in NEAR:
            send_q(queries(e, 0), e, d, 6 + d, 0, d)
        arrived(d_land.at[e * NX], d_sem.at[3 + e])
        for d in NEAR:
            send_d(e * NX, d, e, 6 + e, d, 0)
    land(0)
    for d, far, hop, mid, h in ((2, 3, 1, 2, 0), (6, 5, 7, 6, 1)):
        arrived(kv_at(AT[d]), kv_sem.at[AT[d]])
        send_kv(kv_at(AT[d]), far, hop)
        src, dst = kv.at[h, rows(AT[d])], kv.at[h, rows(AT[4])]
        send(src, dst, 2, kv_sem.at[AT[4]], at_z(mid))
    ks = pl.ds(B * PAIR, PAIR)
    kt[:, ks] = kv[0, ks].T
    tile(PAIR, PAIR, 0, HALF)
    keys_ready(A)
    tile(0, PAIR, 0, HALF)
    land_other(0)
    near_tile(0, 1)
    land(3)
    near_tile(3, 0)
    land(1)
    land(2)
    keys_ready(D)
    keys_ready(C)
    near_tile(2, 0)
    far_tile(D, 0, 1)
    far_tile(C, 0, 1)
    to_sibling(0)
    land_other(3)
    land_other(1)
    land_other(2)
    far_tile(D, 1, 3)
    to_owner(D)
    near_tile(2, 1)
    far_tile(C, 2, 1)
    far_tile(C, 1, 1)
    to_sibling(2)
    queries_done(0)
    far_tile(C, 3, 1)
    near_tile(3, 1)
    to_owner(C)
    to_sibling(3)
    queries_done(2)
    near_tile(1, 1)
    to_sibling(1)
    queries_done(3)
    near_tile(1, 0)
    to_owner(B)
    to_owner(A)
    queries_done(1)
    dq = partial(0, 0, 0) + sib_in[0].astype(F32)
    for dy in (0, 3, 2, 1):
        for s in range(dy * NX, dy * NX + NX):
            if s:
                arrived(dq_in.at[s], dq_sem.at[s])
                dq += dq_in[s].astype(F32)
    out_ref[0] = (dq.T * FACTOR).astype(BF16)
    dk, dv = dk_acc[rows(0)], dv_acc[rows(0)]
    for p in (6, 7, 4, 5, 1, 2, 3):
        arrived(z_in.at[p], z_sem.at[p])
        dk += z_in[p, 0].astype(F32)
        dv += z_in[p, 1].astype(F32)
    out_ref[1] = (dk * FACTOR).astype(BF16)
    out_ref[2] = dv.astype(BF16)
    of(q_all.at[pl.ds(0, 31 * TOK)], 0, q_sem.at[0]).wait_send()
    of(d_land.at[pl.ds(1, 31)], 1, q_sem.at[0]).wait_send()
    of(kv.at[:, pl.ds(0, 7 * TOK)], 2, q_sem.at[0]).wait_send()
    of(z_out.at[pl.ds(1, 7)], 3, q_sem.at[0]).wait_send()
    of(sib_out, 4, q_sem.at[0]).wait_send()
    of(dq_out.at[pl.ds(1, 15)], 5, q_sem.at[0]).wait_send()


def on_device(*args):
    vmem, dma = pltpu.VMEM, pltpu.SemaphoreType.DMA
    blocks = NX * NY
    out = pl.pallas_call(
        kernel,
        out_shape=jax.ShapeDtypeStruct((3, TOK, HEAD), BF16),
        in_specs=[pl.BlockSpec(memory_space=pltpu.HBM)] * 6,
        out_specs=pl.BlockSpec(memory_space=pltpu.VMEM),
        scratch_shapes=[
            vmem((2 * blocks, TOK + AUX, HEAD), BF16),
            vmem((2, KEYS, HEAD), BF16),
            vmem((TOK, HEAD), BF16),
            vmem((TOK,), BF16),
            vmem((QUERIES, HEAD), BF16),
            vmem((QUERIES, HEAD), BF16),
            vmem((HEAD, KEYS), BF16),
            vmem((1, QUERIES), F32),
            vmem((1, QUERIES), F32),
            vmem((HEAD, QUERIES), F32),
            vmem((KEYS, HEAD), F32),
            vmem((KEYS, HEAD), F32),
            vmem((NZ, 2, TOK, HEAD), BF16),
            vmem((NZ, 2, TOK, HEAD), BF16),
            vmem((blocks, HEAD, TOK), BF16),
            vmem((blocks, HEAD, TOK), BF16),
            vmem((blocks, HEAD, TOK), BF16),
            vmem((blocks, HEAD, TOK), BF16),
            dma((6,)),
            dma((6,)),
            dma((14,)),
            dma((14,)),
            dma((NZ,)),
            dma((NY,)),
            dma((NZ,)),
            dma((blocks,)),
        ],
        compiler_params=pltpu.CompilerParams(
            collective_id=0, has_side_effects=True, vmem_limit_bytes=62 << 20
        ),
        name="attention_backward",
    )(*args)
    return out[0], out[1], out[2]


def solution(mesh):
    tokens = P("ctx", None)
    return jax.shard_map(
        on_device,
        mesh=mesh,
        in_specs=(tokens,) * 5 + (P("ctx"),),
        out_specs=(tokens,) * 3,
        check_vma=False,
    )
```

time: 44.5 us -> 41 us (0.921)
  Pallas kernels: 42.3 us -> 38.8 us
    pallas_call x1, Pallas kernels: 42.3 us -> 38.8 us  [on_device(): pl.pallas_call(kernel, out_shape=jax.ShapeDtypeStruct((3, TOK, HEAD), BF1...]
where the time goes in v3:
time: 41 us; the launch traced here: 40.9 us
  Pallas kernels  38.8 us (95%)
  local copies, waits for them, and re-layouts  1.43 us (3%)
  between operations  0.64 us (2%)
    pallas_call x1, Pallas kernels, on_device(): pl.pallas_call(kernel, out_shape=jax.ShapeDtypeStruct((3, TOK, HEAD), BF1...  38.8 us
    squeeze x1, local copies, waits for them, and re-layouts, on_device(): return (out[0], out[1], out[2])  1.43 us

profile of v3, /device:TPU:1, one launch (start us, length us, event | category | flops | bytes accessed | tf_op | source)
XLA Modules:
  0.0 40.9 jit_solution(5769722852131448217)
XLA Ops:
  0.6 38.8 %attention_backward.1 = bf16[3,128,128]{2,1,0:T(8,128)(2,1)} custom-call(bf16[128,128]{1,0:T(8,128)(2,1)} %q_ref.1, bf16[128,128]{1,0:T(8,128)(2,1)} %k_ref.1, bf16[128,128]{1,0:T(8,128)(2,1)} %v_ref.1, bf16[128,128]{1,0:T(8,128)(2,1)} %so_ref.1, bf16[128,128]{1,0:T(8,128)(2,1)} %do_ref.1, bf16[128]{0:T(256)(128)(2,1)} %lse_ref.1), custom_call_target="tpu_custom_call" | custom-call | tf_op jit(solution)/shard_map/attention_backward/pallas_call | solution.py:294
  39.5 1.4 %slice_bitcast_fusion = (bf16[128,128]{1,0:T(8,128)(2,1)}, bf16[128,128]{1,0:T(8,128)(2,1)}, bf16[128,128]{1,0:T(8,128)(2,1)}) fusion(bf16[3,128,128]{2,1,0:T(8,128)(2,1)} %attention_backward.1), kind=kLoop, calls=%fused_computation | loop fusion | bytes 196608 | tf_op jit(solution)/shard_map/squeeze | solution.py:332

commit v4 on v3

--- a/solution.py
+++ b/solution.py
@@ -25,7 +25,7 @@
 AT = {d: p for p, d in enumerate(Z_ORDER)}
 A, B, C, D = range(4)
 NEAR = (1, 3, 2)
-ROW_AT = (0, 3, 2, 1)
+HALF_AT = ((0, 4, 3, 2), (1, 7, 6, 5))
 
 
 def dot(a, b):
@@ -101,11 +101,14 @@
     def kv_at(p):
         return kv.at[:, rows(p)]
 
+    def kv_arrival(p):
+        return kv_sem.at[p if p < 4 else p // 2 + 2]
+
     def send_kv(src, d, dz):
-        send(src, kv_at(AT[d]), 2, kv_sem.at[AT[d]], at_z(dz))
+        send(src, kv_at(AT[d]), 2, kv_arrival(AT[d]), at_z(dz))
 
     def queries(dx, dy, other=0, n=1):
-        return q_all.at[pl.ds(ROW_AT[dy] * ROW + other * HALF + dx * TOK, n * TOK)]
+        return q_all.at[pl.ds(HALF_AT[other][dy] * HALF + dx * TOK, n * TOK)]
 
     def send_q(src, dx, dy, sem, hx, hy):
         send(src, queries(dx, dy), 0, q_sem.at[sem], at_xy(hx, hy))
@@ -115,7 +118,7 @@
 
     for d in (2, 6, 1, 7):
         for h, src in enumerate((k_ref, v_ref)):
-            send(src, kv.at[h, rows(AT[d])], 2, kv_sem.at[AT[d]], at_z(d))
+            send(src, kv.at[h, rows(AT[d])], 2, kv_arrival(AT[d]), at_z(d))
     for d in NEAR:
         send_q(q_ref, d, 0, d, d, 0)
     for i in (1, 2, 3):
@@ -126,9 +129,9 @@
     first = lax.broadcasted_iota(jnp.int32, (AUX, TOK), 0) == 0
     d_land[0, pl.ds(TOK, AUX)] = jnp.where(first, lse_row, delta_row).astype(BF16)
     for d in NEAR:
-        send_d(0, 0, d, 3 + d, 0, d)
+        send_d(0, 0, d, d, 0, d)
     for d in NEAR:
-        send_d(0, d, 0, d, d, 0)
+        send_d(0, d, 0, 4, d, 0)
         send_q(q_ref, 0, d, 3 + d, 0, d)
     fetch[0].wait()
     fetch[4].wait()
@@ -143,7 +146,7 @@
     def take(dy, other):
         for s in range(NX):
             block = other * NX * NY + dy * NX + s
-            to = pl.ds(ROW_AT[dy] * ROW + other * HALF + s * TOK, TOK)
+            to = pl.ds(HALF_AT[other][dy] * HALF + s * TOK, TOK)
             d_all[to] = d_land[block, pl.ds(0, TOK)]
             aux = d_land[block, pl.ds(TOK, AUX)].astype(F32)
             lse_all[:, to] = aux[0:1] * LOG2E
@@ -151,26 +154,32 @@
 
     def land(dy):
         if dy:
-            arrived(queries(0, dy), q_sem.at[3 + dy])
-            arrived(queries(1, dy, 0, 3), q_sem.at[6 + dy])
-            arrived(d_land.at[pl.ds(dy * NX + 1, 3)], d_sem.at[6 + dy])
+            arrived(queries(0, dy, 0, NX), q_sem.at[3 + dy])
+            arrived(d_land.at[pl.ds(dy * NX + 1, 3)], d_sem.at[4 + dy])
         else:
-            for e in NEAR:
-                arrived(d_land.at[e], d_sem.at[e])
-        send(queries(0, dy, 0, NX), queries(0, dy, 1, NX), 0, q_sem.at[10 + dy], sibling)
-        send(d_land.at[row(dy, 0)], d_land.at[row(dy, 1)], 1, d_sem.at[10 + dy], sibling)
+            arrived(d_land.at[pl.ds(1, 3)], d_sem.at[4])
+        sem = 7 if dy == 0 else 8
+        send(queries(0, dy, 0, NX), queries(0, dy, 1, NX), 0, q_sem.at[sem], sibling)
+        send(d_land.at[row(dy, 0)], d_land.at[row(dy, 1)], 1, d_sem.at[sem + 1], sibling)
         take(dy, 0)
 
-    def land_other(dy):
-        arrived(queries(0, dy, 1, NX), q_sem.at[10 + dy])
-        arrived(d_land.at[row(dy, 1)], d_sem.at[10 + dy])
-        take(dy, 1)
+    def land_other_0():
+        arrived(queries(0, 0, 1, NX), q_sem.at[7])
+        arrived(d_land.at[row(0, 1)], d_sem.at[8])
+        take(0, 1)
+
+    def land_other_rest():
+        arrived(queries(0, 3, 1, 3 * NX), q_sem.at[8])
+        arrived(d_land.at[pl.ds(NX * NY + NX, 3 * NX)], d_sem.at[9])
+        for dy in (3, 2, 1):
+            take(dy, 1)
 
     def keys_ready(g):
-        for p in (2 * g, 2 * g + 1):
-            if p:
-                arrived(kv_at(p), kv_sem.at[p])
         ks = pl.ds(g * PAIR, PAIR)
+        if g >= C:
+            arrived(kv.at[:, ks], kv_sem.at[2 + g])
+        else:
+            arrived(kv_at(1), kv_sem.at[1])
         kt[:, ks] = kv[0, ks].T
 
     def tile(k0, kn, q0, qn):
@@ -184,20 +193,24 @@
         dq_acc[:, qs] += dot(kt[:, ks], grads)
 
     def near_tile(dy, other):
-        tile(0, 2 * PAIR, ROW_AT[dy] * ROW + other * HALF, HALF)
-
-    def far_tile(g, first, n):
-        tile(g * PAIR, PAIR, first * ROW, n * ROW)
+        tile(0, 2 * PAIR, HALF_AT[other][dy] * HALF, HALF)
+
+    def far_tile(g, dy):
+        if dy == 0:
+            tile(g * PAIR, PAIR, 0, ROW)
+        else:
+            for other in range(2):
+                tile(g * PAIR, PAIR, HALF_AT[other][dy] * HALF, HALF)
 
     def to_owner(g):
         for p in (2 * g, 2 * g + 1):
             if p:
                 z_out[p, 0] = dk_acc[rows(p)].astype(BF16)
                 z_out[p, 1] = dv_acc[rows(p)].astype(BF16)
-                send(z_out.at[p], z_in.at[p], 3, z_sem.at[p], at_z(NZ - Z_ORDER[p]))
+                send(z_out.at[p], z_in.at[p], 3, z_sem.at[p // 4], at_z(NZ - Z_ORDER[p]))
 
     def partial(dy, other, dx):
-        return dq_acc[:, pl.ds(ROW_AT[dy] * ROW + other * HALF + dx * TOK, TOK)]
+        return dq_acc[:, pl.ds(HALF_AT[other][dy] * HALF + dx * TOK, TOK)]
 
     def to_sibling(dy):
         for dx in range(NX):
@@ -212,72 +225,71 @@
             s = dy * NX + dx
             if s:
                 dq_out[s] = (partial(dy, 0, dx) + sib_in[s].astype(F32)).astype(BF16)
-                send(dq_out.at[s], dq_in.at[s], 5, dq_sem.at[s], at_xy((NX - dx) % NX, (NY - dy) % NY))
+                send(dq_out.at[s], dq_in.at[s], 5, dq_sem.at[min(dy, 2)], at_xy((NX - dx) % NX, (NY - dy) % NY))
 
     for e in NEAR:
         arrived(queries(e, 0), q_sem.at[e])
         for d in NEAR:
-            send_q(queries(e, 0), e, d, 6 + d, 0, d)
-        arrived(d_land.at[e * NX], d_sem.at[3 + e])
+            send_q(queries(e, 0), e, d, 3 + d, 0, d)
+        arrived(d_land.at[e * NX], d_sem.at[e])
         for d in NEAR:
-            send_d(e * NX, d, e, 6 + e, d, 0)
+            send_d(e * NX, d, e, 4 + e, d, 0)
     land(0)
     for d, far, hop, mid, h in ((2, 3, 1, 2, 0), (6, 5, 7, 6, 1)):
         arrived(kv_at(AT[d]), kv_sem.at[AT[d]])
         send_kv(kv_at(AT[d]), far, hop)
         src, dst = kv.at[h, rows(AT[d])], kv.at[h, rows(AT[4])]
-        send(src, dst, 2, kv_sem.at[AT[4]], at_z(mid))
+        send(src, dst, 2, kv_arrival(AT[4]), at_z(mid))
     ks = pl.ds(B * PAIR, PAIR)
     kt[:, ks] = kv[0, ks].T
     tile(PAIR, PAIR, 0, HALF)
     keys_ready(A)
     tile(0, PAIR, 0, HALF)
-    land_other(0)
+    land_other_0()
     near_tile(0, 1)
     land(3)
-    near_tile(3, 0)
     land(1)
     land(2)
     keys_ready(D)
+    near_tile(3, 0)
+    near_tile(2, 0)
+    far_tile(D, 0)
+    tile(D * PAIR, PAIR, 2 * HALF, 3 * HALF)
+    land_other_rest()
     keys_ready(C)
-    near_tile(2, 0)
-    far_tile(D, 0, 1)
-    far_tile(C, 0, 1)
-    to_sibling(0)
-    land_other(3)
-    land_other(1)
-    land_other(2)
-    far_tile(D, 1, 3)
+    tile(D * PAIR, PAIR, 5 * HALF, 3 * HALF)
     to_owner(D)
     near_tile(2, 1)
-    far_tile(C, 2, 1)
-    far_tile(C, 1, 1)
+    far_tile(C, 2)
     to_sibling(2)
+    far_tile(C, 3)
+    far_tile(C, 1)
+    far_tile(C, 0)
+    to_owner(C)
+    to_sibling(0)
+    queries_done(2)
+    near_tile(3, 1)
+    near_tile(1, 1)
+    to_sibling(3)
+    to_sibling(1)
     queries_done(0)
-    far_tile(C, 3, 1)
-    near_tile(3, 1)
-    to_owner(C)
-    to_sibling(3)
-    queries_done(2)
-    near_tile(1, 1)
-    to_sibling(1)
-    queries_done(3)
     near_tile(1, 0)
     to_owner(B)
     to_owner(A)
+    queries_done(3)
     queries_done(1)
     dq = partial(0, 0, 0) + sib_in[0].astype(F32)
-    for dy in (0, 3, 2, 1):
-        for s in range(dy * NX, dy * NX + NX):
-            if s:
-                arrived(dq_in.at[s], dq_sem.at[s])
-                dq += dq_in[s].astype(F32)
+    for sem, first, n in ((0, 1, 3), (2, 8, 8), (1, 4, 4)):
+        arrived(dq_in.at[pl.ds(first, n)], dq_sem.at[sem])
+        for s in range(first, first + n):
+            dq += dq_in[s].astype(F32)
     out_ref[0] = (dq.T * FACTOR).astype(BF16)
     dk, dv = dk_acc[rows(0)], dv_acc[rows(0)]
-    for p in (6, 7, 4, 5, 1, 2, 3):
-        arrived(z_in.at[p], z_sem.at[p])
-        dk += z_in[p, 0].astype(F32)
-        dv += z_in[p, 1].astype(F32)
+    for sem, first, n in ((1, 4, 4), (0, 1, 3)):
+        arrived(z_in.at[pl.ds(first, n)], z_sem.at[sem])
+        for p in range(first, first + n):
+            dk += z_in[p, 0].astype(F32)
+            dv += z_in[p, 1].astype(F32)
     out_ref[1] = (dk * FACTOR).astype(BF16)
     out_ref[2] = dv.astype(BF16)
     of(q_all.at[pl.ds(0, 31 * TOK)], 0, q_sem.at[0]).wait_send()
@@ -317,12 +329,12 @@
             vmem((blocks, HEAD, TOK), BF16),
             dma((6,)),
             dma((6,)),
-            dma((14,)),
-            dma((14,)),
-            dma((NZ,)),
+            dma((9,)),
+            dma((10,)),
+            dma((6,)),
             dma((NY,)),
-            dma((NZ,)),
-            dma((blocks,)),
+            dma((2,)),
+            dma((3,)),
         ],
         compiler_params=pltpu.CompilerParams(
             collective_id=0, has_side_effects=True, vmem_limit_bytes=62 << 20

time: 41 us -> 39.3 us (0.959)
  Pallas kernels: 38.8 us -> 37.1 us
    pallas_call x1, Pallas kernels: 38.8 us -> 37.1 us  [on_device(): pl.pallas_call(kernel, out_shape=jax.ShapeDtypeStruct((3, TOK, HEAD), BF1...]
where the time goes in v4:
time: 39.3 us; the launch traced here: 39.2 us
  Pallas kernels  37.1 us (94%)
  local copies, waits for them, and re-layouts  1.43 us (4%)
  between operations  0.64 us (2%)
    pallas_call x1, Pallas kernels, on_device(): pl.pallas_call(kernel, out_shape=jax.ShapeDtypeStruct((3, TOK, HEAD), BF1...  37.1 us
    squeeze x1, local copies, waits for them, and re-layouts, on_device(): return (out[0], out[1], out[2])  1.43 us

profile of v4, /device:TPU:1, one launch (start us, length us, event | category | flops | bytes accessed | tf_op | source)
XLA Modules:
  0.0 39.2 jit_solution(20757702904609759)
XLA Ops:
  0.6 37.1 %attention_backward.1 = bf16[3,128,128]{2,1,0:T(8,128)(2,1)} custom-call(bf16[128,128]{1,0:T(8,128)(2,1)} %q_ref.1, bf16[128,128]{1,0:T(8,128)(2,1)} %k_ref.1, bf16[128,128]{1,0:T(8,128)(2,1)} %v_ref.1, bf16[128,128]{1,0:T(8,128)(2,1)} %so_ref.1, bf16[128,128]{1,0:T(8,128)(2,1)} %do_ref.1, bf16[128]{0:T(256)(128)(2,1)} %lse_ref.1), custom_call_target="tpu_custom_call" | custom-call | tf_op jit(solution)/shard_map/attention_backward/pallas_call | solution.py:306
  37.7 1.4 %slice_bitcast_fusion = (bf16[128,128]{1,0:T(8,128)(2,1)}, bf16[128,128]{1,0:T(8,128)(2,1)}, bf16[128,128]{1,0:T(8,128)(2,1)}) fusion(bf16[3,128,128]{2,1,0:T(8,128)(2,1)} %attention_backward.1), kind=kLoop, calls=%fused_computation | loop fusion | bytes 196608 | tf_op jit(solution)/shard_map/squeeze | solution.py:344

commit v5 on v4

--- a/solution.py
+++ b/solution.py
@@ -43,7 +43,7 @@
 def kernel(
     q_ref, k_ref, v_ref, so_ref, do_ref, lse_ref, out_ref,
     d_land, kv, so_buf, lse_buf, q_all, d_all, kt, lse_all, delta_all,
-    dq_acc, dk_acc, dv_acc, z_out, z_in, sib_out, sib_in, dq_out, dq_in,
+    dq_acc, dk_acc, dv_acc, z_out, z_in, sib_out, sib_in, dq_out, dq_in, out_buf,
     local_sem, send_sem, q_sem, d_sem, kv_sem, sib_sem, z_sem, dq_sem,
 ):
     me = lax.axis_index("ctx")
@@ -278,26 +278,35 @@
     to_owner(A)
     queries_done(3)
     queries_done(1)
+    def add_keys(dk, dv, sem, first, n):
+        arrived(z_in.at[pl.ds(first, n)], z_sem.at[sem])
+        for p in range(first, first + n):
+            dk += z_in[p, 0].astype(F32)
+            dv += z_in[p, 1].astype(F32)
+        return dk, dv
+
+    dk, dv = add_keys(dk_acc[rows(0)], dv_acc[rows(0)], 1, 4, 4)
     dq = partial(0, 0, 0) + sib_in[0].astype(F32)
     for sem, first, n in ((0, 1, 3), (2, 8, 8), (1, 4, 4)):
         arrived(dq_in.at[pl.ds(first, n)], dq_sem.at[sem])
         for s in range(first, first + n):
             dq += dq_in[s].astype(F32)
-    out_ref[0] = (dq.T * FACTOR).astype(BF16)
-    dk, dv = dk_acc[rows(0)], dv_acc[rows(0)]
-    for sem, first, n in ((1, 4, 4), (0, 1, 3)):
-        arrived(z_in.at[pl.ds(first, n)], z_sem.at[sem])
-        for p in range(first, first + n):
-            dk += z_in[p, 0].astype(F32)
-            dv += z_in[p, 1].astype(F32)
-    out_ref[1] = (dk * FACTOR).astype(BF16)
-    out_ref[2] = dv.astype(BF16)
+    out_buf[0] = (dq.T * FACTOR).astype(BF16)
+    write_queries = pltpu.make_async_copy(out_buf.at[0], out_ref.at[0], local_sem.at[0])
+    write_queries.start()
+    dk, dv = add_keys(dk, dv, 0, 1, 3)
+    out_buf[1] = (dk * FACTOR).astype(BF16)
+    out_buf[2] = dv.astype(BF16)
+    write_keys = pltpu.make_async_copy(out_buf.at[pl.ds(1, 2)], out_ref.at[pl.ds(1, 2)], local_sem.at[1])
+    write_keys.start()
     of(q_all.at[pl.ds(0, 31 * TOK)], 0, q_sem.at[0]).wait_send()
     of(d_land.at[pl.ds(1, 31)], 1, q_sem.at[0]).wait_send()
     of(kv.at[:, pl.ds(0, 7 * TOK)], 2, q_sem.at[0]).wait_send()
     of(z_out.at[pl.ds(1, 7)], 3, q_sem.at[0]).wait_send()
     of(sib_out, 4, q_sem.at[0]).wait_send()
     of(dq_out.at[pl.ds(1, 15)], 5, q_sem.at[0]).wait_send()
+    write_queries.wait()
+    write_keys.wait()
 
 
 def on_device(*args):
@@ -307,7 +316,7 @@
         kernel,
         out_shape=jax.ShapeDtypeStruct((3, TOK, HEAD), BF16),
         in_specs=[pl.BlockSpec(memory_space=pltpu.HBM)] * 6,
-        out_specs=pl.BlockSpec(memory_space=pltpu.VMEM),
+        out_specs=pl.BlockSpec(memory_space=pltpu.HBM),
         scratch_shapes=[
             vmem((2 * blocks, TOK + AUX, HEAD), BF16),
             vmem((2, KEYS, HEAD), BF16),
@@ -327,6 +336,7 @@
             vmem((blocks, HEAD, TOK), BF16),
             vmem((blocks, HEAD, TOK), BF16),
             vmem((blocks, HEAD, TOK), BF16),
+            vmem((3, TOK, HEAD), BF16),
             dma((6,)),
             dma((6,)),
             dma((9,)),

time: 39.3 us -> 39.3 us (level)
  no operation moved by 1% of the time
where the time goes in v5:
time: 39.3 us; the launch traced here: 39.1 us
  Pallas kernels  37.1 us (94%)
  local copies, waits for them, and re-layouts  1.43 us (4%)
  between operations  0.64 us (2%)
    pallas_call x1, Pallas kernels, on_device(): pl.pallas_call(kernel, out_shape=jax.ShapeDtypeStruct((3, TOK, HEAD), BF1...  37.1 us
    squeeze x1, local copies, waits for them, and re-layouts, on_device(): return (out[0], out[1], out[2])  1.43 us

profile of v5, /device:TPU:1, one launch (start us, length us, event | category | flops | bytes accessed | tf_op | source)
XLA Modules:
  0.0 39.1 jit_solution(17499886850804202356)
XLA Ops:
  0.6 37.1 %attention_backward.1 = bf16[3,128,128]{2,1,0:T(8,128)(2,1)} custom-call(bf16[128,128]{1,0:T(8,128)(2,1)} %q_ref.1, bf16[128,128]{1,0:T(8,128)(2,1)} %k_ref.1, bf16[128,128]{1,0:T(8,128)(2,1)} %v_ref.1, bf16[128,128]{1,0:T(8,128)(2,1)} %so_ref.1, bf16[128,128]{1,0:T(8,128)(2,1)} %do_ref.1, bf16[128]{0:T(256)(128)(2,1)} %lse_ref.1), custom_call_target="tpu_custom_call" | custom-call | tf_op jit(solution)/shard_map/attention_backward/pallas_call | solution.py:315
  37.7 1.4 %slice_bitcast_fusion = (bf16[128,128]{1,0:T(8,128)(2,1)}, bf16[128,128]{1,0:T(8,128)(2,1)}, bf16[128,128]{1,0:T(8,128)(2,1)}) fusion(bf16[3,128,128]{2,1,0:T(8,128)(2,1)} %attention_backward.1), kind=kLoop, calls=%fused_computation | loop fusion | bytes 196608 | tf_op jit(solution)/shard_map/squeeze | solution.py:354
